TPU v7x, 256 devices: a whole 4x4x8 slice. The times are simulated.
256 devices in a mesh: pair: 64 (over x, z, core), fock: 4 (over y).
Axes of the slice: x: 4, y: 4, z: 8, core: 2. Of those that a mesh axis runs over, the one named last changes fastest.
Arguments:
- three_center: bfloat16 [3072, 64, 4096], P('pair', 'fock'), may hold values from -0.75 to 0.75
- coefficients: bfloat16 [32, 19968], replicated, may hold values from -0.23925781 to 0.23925781
- metric_inv: bfloat16 [512, 512], replicated, as said below
- target_owner: int32 [3072, 1], P('pair'), may hold values from 0 to 63; in each aligned block of 48 rows (0 to 47, 48 to 95, ...) at most 2 rows name the same one
- row_slot: int32 [3072], P('pair'), may hold values from 0 to 7
- aux_block: int32 [3072], P('pair'), may hold values from 0 to 7
- ao_block: int32 [3072], P('pair'), may hold values from 0 to 311
Outputs:
- exchange: bfloat16 [32768, 512], P(('pair', 'fock'))
Inputs may be any that keep to these rules, and one draw needn't show every extreme that they name: `target_owner`: among the 48 blocks of one index of pair, no owner is named more than 2 times; some owner is named exactly 2 times. `metric_inv`: symmetric.
All inputs are finite; a program needn't handle non-finite values.
Results may differ from a plain program's by a relative error of at most 0.0033.
Values may be sent and summed in bfloat16 or wider, within the bound.
No kernel may reach another device: no remote copies, remote signals or barrier semaphores. Data moves between devices by JAX's collectives and lax.ppermute only.
A program may use at most 128 MiB of HBM per device.

v0:
```python
import functools

import jax
import jax.numpy as jnp
from jax import lax
from jax.experimental import pallas as pl
from jax.experimental.pallas import tpu as pltpu
from jax.sharding import Mesh, PartitionSpec as P

BLK = 64
AUXB = 8
ROWB = 8
NAUX = 512
LANES = 128
SLOTS = 4
MAIN = 3
GROUP = 12
PARTS = 4
FETCH = 4
AXES = ("x", "z", "c", "y")
AWAY = ("c", "x", "y", "z")


def units_kernel(
    owner_ref, row_ref, aux_ref, ao_ref, three_ref, coef_ref,
    main_ref, extra_ref, tag_ref, rows_ref, made_ref, held_ref, spread_ref, chip_ref, slot_ref, got, sent
):
    count, _, depth_in = rows_ref.shape
    tiles = depth_in // LANES
    depth = tiles * 8
    orbitals = coef_ref.shape[0]
    chips, columns = tag_ref.shape
    depths = main_ref.shape[3]

    def fetch(step):
        units = pl.ds(step * FETCH, FETCH)
        return pltpu.make_async_copy(three_ref.at[units], rows_ref.at[units], got.at[step])

    orbitals_held = pltpu.make_async_copy(coef_ref, held_ref, got.at[count // FETCH])
    orbitals_held.start()

    def send(unit, act):
        chip, slot = chip_ref[unit], slot_ref[unit]
        across, along = chip // depths, chip % depths

        @pl.when(slot < MAIN)
        def _():
            act(pltpu.make_async_copy(made_ref.at[unit], main_ref.at[:, across, :, along, slot], sent.at[unit]))

        @pl.when(slot >= MAIN)
        def _():
            act(pltpu.make_async_copy(made_ref.at[unit], extra_ref.at[:, across, :, along, 0], sent.at[unit]))

    for step in range(count // FETCH):
        fetch(step).start()

    held = lax.broadcasted_iota(jnp.int32, (LANES, 2 * depth), 0)
    column = lax.broadcasted_iota(jnp.int32, (LANES, 2 * depth), 1)
    source = 2 * (column % depth // 8) + column // depth
    for half in range(2):
        spread_ref[half] = jnp.where(held == half * BLK + source, 1.0, 0.0).astype(jnp.bfloat16)

    def clear(chip, carry):
        for k in range(columns):
            tag_ref[chip, k] = -1 if k < SLOTS else 0
        return carry

    lax.fori_loop(0, chips, clear, 0)

    def rank(unit, fullest):
        owner = owner_ref[unit]
        chip = owner // 2
        slot = tag_ref[chip, SLOTS]
        chip_ref[unit] = chip
        slot_ref[unit] = slot
        tag_ref[chip, slot] = owner % 2 * (ROWB * AUXB) + row_ref[unit] * AUXB + aux_ref[unit]
        tag_ref[chip, SLOTS] = slot + 1
        return jnp.maximum(fullest, slot + 1)

    fullest = lax.fori_loop(0, count, rank, 0)

    def note(chip, carry):
        tag_ref[chip, SLOTS] = fullest
        return carry

    lax.fori_loop(0, chips, note, 0)

    lane = lax.broadcasted_iota(jnp.int32, (orbitals, 8, depth), 2)
    row = lax.broadcasted_iota(jnp.int32, (orbitals, 8, depth), 1)
    keep = (lane & 7) == row
    low = lax.broadcasted_iota(jnp.int32, (orbitals // 2, 8, LANES), 2) < BLK

    orbitals_held.wait()

    def group(step, carry):
        for k in range(GROUP // FETCH):
            fetch(step * (GROUP // FETCH) + k).wait()
        spreads = []
        for k in range(GROUP):
            ao = ao_ref[step * GROUP + k]
            picked = held_ref[:, pl.ds(pl.multiple_of(ao // 2 * LANES, LANES), LANES)]
            spreads.append(jnp.dot(picked, spread_ref[ao % 2], preferred_element_type=jnp.float32))
        for k in range(GROUP):
            rows = rows_ref[step * GROUP + k].astype(jnp.float32)
            stacked = [
                jnp.concatenate([rows[h * 8 : h * 8 + 8, j * LANES : (j + 1) * LANES] for j in range(tiles)], axis=0)
                for h in range(2)
            ]
            right = jnp.concatenate(stacked, axis=1).astype(jnp.bfloat16)
            parts = []
            for parity in range(2):
                wide = spreads[k][:, None, parity * depth : (parity + 1) * depth]
                wide = jnp.broadcast_to(wide, (orbitals, 8, depth))
                left = jnp.where(keep, wide, 0.0).reshape(orbitals * 8, depth).astype(jnp.bfloat16)
                made = jnp.dot(left, right, preferred_element_type=jnp.float32)
                parts.append(made.reshape(orbitals // 2, 2, 8, 2 * LANES))
            done = []
            for h in range(2):
                cut = slice(h * LANES, (h + 1) * LANES)
                stay = jnp.where(low, parts[0][:, 0, :, cut], parts[1][:, 1, :, cut])
                move = jnp.where(low, parts[0][:, 1, :, cut], parts[1][:, 0, :, cut])
                done.append(stay + pltpu.roll(move, BLK, 2))
            units = jnp.stack(done, axis=1).reshape(orbitals * 8, LANES).astype(jnp.bfloat16)
            made_ref[step * GROUP + k] = units.reshape(2, 4, orbitals, LANES)
        for k in range(GROUP):
            send(step * GROUP + k, lambda copy: copy.start())
        return carry

    lax.fori_loop(0, count // GROUP, group, 0)
    for unit in range(count):
        send(unit, lambda copy: copy.wait())


def make_units(three_center, coefficients, owner, row_slot, aux_block, ao_block, chips):
    count, rows, depth = three_center.shape
    orbitals = coefficients.shape[0]
    across, along = chips
    scalars = pl.BlockSpec(memory_space=pltpu.SMEM)
    main = (2, across, 4, along, MAIN, orbitals, LANES)
    extra = (2, across, 4, along, SLOTS - MAIN, orbitals, LANES)
    return pl.pallas_call(
        units_kernel,
        in_specs=[scalars] * 4
        + [pl.BlockSpec(memory_space=pltpu.HBM)] * 2,
        out_specs=[pl.BlockSpec(memory_space=pltpu.HBM)] * 2 + [scalars],
        out_shape=[
            jax.ShapeDtypeStruct(main, jnp.bfloat16),
            jax.ShapeDtypeStruct(extra, jnp.bfloat16),
            jax.ShapeDtypeStruct((across * along, 8), jnp.int32),
        ],
        scratch_shapes=[
            pltpu.VMEM((count, rows, depth), jnp.bfloat16),
            pltpu.VMEM((count, 2, 4, orbitals, LANES), jnp.bfloat16),
            pltpu.VMEM(coefficients.shape, jnp.bfloat16),
            pltpu.VMEM((2, LANES, BLK * 8), jnp.bfloat16),
            pltpu.SMEM((count,), jnp.int32),
            pltpu.SMEM((count,), jnp.int32),
            pltpu.SemaphoreType.DMA((count // FETCH + 1,)),
            pltpu.SemaphoreType.DMA((count,)),
        ],
        compiler_params=pltpu.CompilerParams(vmem_limit_bytes=60 * 1024 * 1024),
        name="units",
    )(owner, row_slot, aux_block, ao_block, three_center, coefficients)


def fit(whole, metric_ref, fitted):
    for orbital in range(2):
        cut = slice(orbital * NAUX, (orbital + 1) * NAUX)
        made = jnp.dot(whole[:, cut], metric_ref[...], preferred_element_type=jnp.float32)
        fitted[:, cut] = made.astype(jnp.bfloat16)


def own_exchange(whole, metric_ref, fitted, out_ref, first):
    fit(whole, metric_ref, fitted)
    part = lax.dot_general(fitted[...], whole, (((1,), (1,)), ((), ())), preferred_element_type=jnp.float32)
    if first:
        out_ref[...] = part
    else:
        out_ref[...] += part


def by_orbital(total, owner, pair):
    low = lax.broadcasted_iota(jnp.int32, total.shape[-2:], 1) < BLK
    lower, upper = [], []
    for aux in range(0, AUXB, 2):
        even, odd = total[owner, pair, aux], total[owner, pair, aux + 1]
        moved = pltpu.roll(jnp.where(low, odd, even), BLK, 1)
        lower.append(jnp.where(low, even, moved).astype(jnp.bfloat16))
        upper.append(jnp.where(low, moved, odd).astype(jnp.bfloat16))
    return lower + upper


def gather_kernel(tag_ref, place_ref, metric_ref, *refs):
    inputs = refs[: len(refs) - 6]
    mine_ref, out_ref, total, fitted, held, got = refs[len(refs) - 6 :]
    groups, quarters, depths, slots = held.shape[:4]
    columns = groups // 2
    planes = groups // PARTS

    def fetch(step):
        part = pl.ds(step * planes, planes)
        copies, first = [], 0
        for index, ref in enumerate(inputs):
            spots = pl.ds(first, ref.shape[3])
            copies.append(pltpu.make_async_copy(ref.at[part], held.at[part, :, :, spots], got.at[index, step]))
            first += ref.shape[3]
        return copies

    for step in range(PARTS):
        for copy in fetch(step):
            copy.start()
    total[...] = jnp.zeros_like(total)

    def add(source, carry):
        group, depth = lax.shift_right_logical(source, 3), source & (depths - 1)
        core, column = lax.shift_right_logical(group, 2), group & (columns - 1)
        away = (place_ref[2] - depth - 1) & (depths - 1)
        away = away ^ (place_ref[0] * (depths // 2))
        away = away * columns + ((place_ref[1] - column) & (columns - 1))
        for slot in range(slots):
            tag = tag_ref[away * 2 + core, slot]

            @pl.when(tag >= 0)
            def _():
                owner, row = lax.shift_right_logical(tag, 6), lax.shift_right_logical(tag, 3) & (ROWB - 1)
                aux = tag & (AUXB - 1)
                spots = [
                    (owner, pair, aux, pl.ds(pl.multiple_of(row * BLK + quarter * 16, 16), 16), slice(None))
                    for quarter in range(quarters)
                    for pair in range(2)
                ]
                news = [
                    held[group, quarter, depth, slot, pair * 16 : pair * 16 + 16, :].astype(jnp.float32)
                    for quarter in range(quarters)
                    for pair in range(2)
                ]
                sums = [total[spot] + new for spot, new in zip(spots, news)]
                for spot, value in zip(spots, sums):
                    total[spot] = value

        return carry

    for step in range(PARTS):
        for copy in fetch(step):
            copy.wait()
        lax.fori_loop(step * planes * depths, (step + 1) * planes * depths, add, 0)

    mine = place_ref[0]
    for pair in range(2):
        whole = jnp.concatenate(by_orbital(total, 1 - mine, pair), axis=1)
        own_exchange(whole, metric_ref, fitted, out_ref, pair == 0)
    for pair in range(2):
        for index, tile in enumerate(by_orbital(total, mine, pair)):
            mine_ref[pair, :, index * LANES : (index + 1) * LANES] = tile


def rest_kernel(place_ref, mine_ref, metric_ref, before_ref, got_ref, *refs):
    outs, fitted, made = refs[:-2], refs[-2], refs[-1]
    own_exchange(mine_ref[1], metric_ref, fitted, made, True)
    share = outs[0].shape[0]
    for away, out_ref in enumerate(outs):
        rows = pl.ds(pl.multiple_of(((place_ref[3] + away) & (len(outs) - 1)) * share, share), share)
        out_ref[...] = made[rows] + before_ref[rows] + got_ref[rows]


def half_kernel(mine_ref, metric_ref, out_ref, fitted):
    own_exchange(mine_ref[0], metric_ref, fitted, out_ref, True)


def gather_exchange(tags, place, incoming, metric):
    groups, quarters, depths, _, rows, lanes = incoming[0].shape
    slots = sum(array.shape[3] for array in incoming)
    width = ROWB * BLK
    inner = AUXB * lanes
    scalars = pl.BlockSpec(memory_space=pltpu.SMEM)
    held = pl.BlockSpec(memory_space=pltpu.VMEM)
    return pl.pallas_call(
        gather_kernel,
        in_specs=[scalars, scalars, held] + [pl.BlockSpec(memory_space=pltpu.HBM)] * len(incoming),
        out_specs=[held, held],
        out_shape=[
            jax.ShapeDtypeStruct((2, width, inner), jnp.bfloat16),
            jax.ShapeDtypeStruct((width, width), jnp.float32),
        ],
        scratch_shapes=[
            pltpu.VMEM((2, 2, AUXB, width, lanes), jnp.float32),
            pltpu.VMEM((width, inner), jnp.bfloat16),
            pltpu.VMEM((groups, quarters, depths, slots, rows, lanes), jnp.bfloat16),
            pltpu.SemaphoreType.DMA((len(incoming), PARTS)),
        ],
        compiler_params=pltpu.CompilerParams(vmem_limit_bytes=40 * 1024 * 1024),
        name="gather_exchange",
    )(tags, place, metric, *incoming)


def half_exchange(mine, metric):
    _, width, inner = mine.shape
    return pl.pallas_call(
        half_kernel,
        out_shape=jax.ShapeDtypeStruct((width, width), jnp.float32),
        scratch_shapes=[pltpu.VMEM((width, inner), jnp.bfloat16)],
        compiler_params=pltpu.CompilerParams(vmem_limit_bytes=40 * 1024 * 1024),
        cost_estimate=pl.CostEstimate(
            flops=2 * width * inner * (inner // 2 + width), bytes_accessed=5 * width * inner * 2, transcendentals=0
        ),
        name="half_exchange",
    )(mine, metric)


def rest_exchange(place, mine, metric, before, got):
    _, width, inner = mine.shape
    held = pl.BlockSpec(memory_space=pltpu.VMEM)
    return pl.pallas_call(
        rest_kernel,
        in_specs=[pl.BlockSpec(memory_space=pltpu.SMEM)] + [held] * 4,
        out_specs=[held] * 4,
        out_shape=[jax.ShapeDtypeStruct((width // 4, width), jnp.float32)] * 4,
        scratch_shapes=[pltpu.VMEM((width, inner), jnp.bfloat16), pltpu.VMEM((width, width), jnp.float32)],
        compiler_params=pltpu.CompilerParams(vmem_limit_bytes=40 * 1024 * 1024),
        name="rest_exchange",
    )(place, mine, metric, before, got)


def part(table, index, axis):
    return lax.dynamic_index_in_dim(table, index, axis, keepdims=False)


def share_tags(tags, across, along):
    core, column, depth = lax.axis_index("c"), lax.axis_index("x"), lax.axis_index("z")
    swap = [(0, 1), (1, 0)]
    first = core == 0
    other = lax.ppermute(tags, "c", swap)
    both = jnp.where(first, jnp.stack([tags, other]), jnp.stack([other, tags])).reshape(2, across, along, 8)
    rows = [part(both, column, 1)]
    for away in range(1, across):
        steps = [(k, (k + away) % across) for k in range(across)]
        rows.append(lax.ppermute(part(both, (column + away) % across, 1), "x", steps))
    table = jnp.stack(rows)
    half = along // 2
    rows = []
    for away in range(1, half + 1):
        steps = [(z * 2 + c, (z + away + half * c) % along * 2 + c) for z in range(along) for c in range(2)]
        rows.append(lax.ppermute(part(table, (depth + away + half * core) % along, 2), ("z", "c"), steps))
    rows = jnp.stack(rows)
    return jnp.stack([rows, lax.ppermute(rows, "c", swap)])


def body(three_center, coefficients, metric_inv, target_owner, row_slot, aux_block, ao_block):
    orbitals = coefficients.shape[0]
    cores, across, along = lax.axis_size("c"), lax.axis_size("x"), lax.axis_size("z")
    main, extra, tags = make_units(
        three_center, coefficients, target_owner[:, 0], row_slot, aux_block, ao_block, (across, along)
    )
    devices = cores * across * 4 * along
    main = main.reshape(devices, MAIN, orbitals, LANES)
    extra = extra.reshape(devices, SLOTS - MAIN, orbitals, LANES)
    main = lax.all_to_all(main, AWAY, split_axis=0, concat_axis=0, tiled=True)

    tags = share_tags(tags, across, along).reshape(cores * across * along, 8)
    place = jnp.stack([lax.axis_index("c"), lax.axis_index("x"), lax.axis_index("z"), lax.axis_index("y")])

    def finish(tags, incoming, place, metric):
        incoming = [array.reshape(cores * across, 4, along, -1, orbitals, LANES) for array in incoming]
        mine, sent = gather_exchange(tags, place, incoming, metric)
        got = lax.ppermute(sent, "c", [(0, 1), (1, 0)])
        return tuple(rest_exchange(place, mine, metric, half_exchange(mine, metric), got))

    def few(main, extra, tags, place, metric):
        return finish(tags, [main], place, metric)

    def many(main, extra, tags, place, metric):
        extra = lax.all_to_all(extra, AWAY, split_axis=0, concat_axis=0, tiled=True)
        return finish(tags, [main, extra], place, metric)

    overflow = jnp.max(tags[:, SLOTS]) > MAIN
    shares = lax.cond(overflow, many, few, main, extra, tags, place, metric_inv)
    total = shares[0]
    for away in (2, 1, 3):
        total += lax.ppermute(shares[away], "y", [(k, (k + away) % 4) for k in range(4)])
    return total.astype(jnp.bfloat16)


def solution(mesh):
    split = Mesh(mesh.devices.reshape(4, 8, 2, 4), AXES)
    pair = ("x", "z", "c")
    in_specs = (P(pair, "y", None), P(), P(), P(pair, None), P(pair), P(pair), P(pair))
    out_specs = P(AXES, None)
    return jax.shard_map(body, mesh=split, in_specs=in_specs, out_specs=out_specs, check_vma=False)
```

profile of v0, /device:TPU:1, one launch (start us, length us, event | category | flops | bytes accessed | tf_op | source)
XLA Modules:
  0.0 199.4 jit_solution(4039567207723123682)
XLA Ops:
  0.0 10.7 %units.1 = (bf16[2,4,4,8,3,32,128]{6,5,4,3,2,1,0:T(8,128)(2,1)}, bf16[2,4,4,8,1,32,128]{6,5,4,3,2,1,0:T(8,128)(2,1)S(1)}, s32[32,8]{1,0:T(8,128)}) custom-call(s32[48]{0:T(128)} %bitcast.65, s32[48]{0:T(128)} %row_ref.1, s32[48]{0:T(128)} %aux_ref.1, s32[48]{0:T(128)} %ao_ref.1, bf16[48,16,4096]{2,1,0:T(8,128)(2,1)} %three_ref.1, bf16[32,19968]{1,0:T(8,128)(2,1)} %coef_ref.1), custom_call_target="tpu_custom_call" | custom-call | tf_op jit(solution)/shard_map/units/pallas_call | solution.py:141
  10.7 0.0 copy-start.1
  10.8 0.0 copy-start
  10.8 16.5 %all-to-all-start.1 = ((bf16[256,3,32,128]{3,2,1,0:T(8,128)(2,1)}), bf16[256,3,32,128]{3,2,1,0:T(8,128)(2,1)}, u32[]{:S(2)}, u32[]{:S(2)}) async-start(bf16[256,3,32,128]{3,2,1,0:T(8,128)(2,1)} %bitcast.42), calls=%async_computation.1 | async-start | bytes 12582912 | tf_op jit(solution)/shard_map/all_to_all | solution.py:357
  27.3 2.3 %collective-permute-start.2 = (s32[32,8]{1,0:T(8,128)S(1)}, s32[32,8]{1,0:T(8,128)S(1)}, u32[]{:S(2)}, u32[]{:S(2)}) collective-permute-start(s32[32,8]{1,0:T(8,128)S(1)} %copy-done.1), channel_id=1, source_target_pairs={{0,4},{4,0},{1,5},{5,1},{2,6},{6,2},{3,7},{7,3},{8,12},{12,8},{9,1... | collective-permute-start | bytes 3080 | tf_op jit(solution)/shard_map/ppermute | solution.py:332
  29.6 0.8 collective-permute-done.2
  30.5 0.8 collective-permute-start.5
  31.3 0.6 collective-permute-start.4
  31.9 0.6 collective-permute-start.3
  32.5 12.2 %collective-permute-done.5 = s32[2,8,8]{2,1,0:T(8,128)S(1)} collective-permute-done((s32[2,8,8]{2,1,0:T(8,128)S(1)}, s32[2,8,8]{2,1,0:T(8,128)S(1)}, u32[]{:S(2)}, u32[]{:S(2)}) %collective-permute-start.5) | collective-permute-done | bytes 544 | tf_op jit(solution)/shard_map/ppermute | solution.py:337
  44.7 0.0 collective-permute-done.4
  44.8 0.7 collective-permute-start.9
  45.4 4.0 %collective-permute-start.6 = (s32[4,2,8]{2,1,0:T(2,128)S(1)}, s32[4,2,8]{2,1,0:T(2,128)S(1)}, u32[]{:S(2)}, u32[]{:S(2)}) collective-permute-start(s32[4,2,8]{2,1,0:T(2,128)S(1)} %bitcast.63), channel_id=1, source_target_pairs={{0,8},{4,44},{8,16},{12,52},{16,24},{20,60},{24,32},{28,4},{32,40}... | collective-permute-start | bytes 776 | tf_op jit(solution)/shard_map/ppermute | solution.py:343
  49.4 1.8 collective-permute-start.8
  51.2 0.1 pad_add_fusion.3
  51.3 110.9 %collective-permute-done.6 = s32[4,2,8]{2,1,0:T(2,128)S(1)} collective-permute-done((s32[4,2,8]{2,1,0:T(2,128)S(1)}, s32[4,2,8]{2,1,0:T(2,128)S(1)}, u32[]{:S(2)}, u32[]{:S(2)}) %collective-permute-start.6) | collective-permute-done | bytes 288 | tf_op jit(solution)/shard_map/ppermute | solution.py:343
  162.3 0.0 collective-permute-done.8
  162.3 5.4 %collective-permute-start.10 = (s32[4,4,2,8]{3,2,1,0:T(2,128)S(1)}, s32[4,4,2,8]{3,2,1,0:T(2,128)S(1)}, u32[]{:S(2)}, u32[]{:S(2)}) collective-permute-start(s32[4,4,2,8]{3,2,1,0:T(2,128)S(1)} %pad_add_fusion.2), channel_id=1, source_target_pairs={{0,4},{4,0},{1,5},{5,1},{2,6},{6,2},{3,7},{7,3},{8,12},{12,8},{9,1... | collective-permute-start | bytes 3080 | tf_op jit(solution)/shard_map/ppermute | solution.py:345
  167.7 0.8 collective-permute-done.10
  168.6 0.7 slice_reduce_fusion
  169.9 13.2 %conditional.1 = ((f32[128,512]{1,0:T(8,128)S(1)}, f32[128,512]{1,0:T(8,128)S(1)}, f32[128,512]{1,0:T(8,128)S(1)}, f32[128,512]{1,0:T(8,128)S(1)})) conditional(s32[]{:T(128)} %convert_element_type.6, (bf16[256,3,32,128]{3,2,1,0:T(8,128)(2,1)}, s32[64,8]{1,0:T(8,128)S(1)}, s32[4]{0:T(128)S(1)}, bf16[512,512]{1,0:T(8,128)(2,1)S(1)}) %tuple.27, ...), branch_computations={%region_1.2_spmd, %region_2.3_spmd} | conditional | flops 1073741824 | bytes 13631536 | solution.py:376
  170.1 8.1 %gather_exchange.2 = (bf16[2,512,1024]{2,1,0:T(8,128)(2,1)S(1)}, f32[512,512]{1,0:T(8,128)S(1)}) custom-call(s32[64,8]{1,0:T(8,128)S(1)} %get-tuple-element.25.tag_ref, s32[4]{0:T(128)S(1)} %get-tuple-element.24.place_ref, bf16[512,512]{1,0:T(8,128)(2,1)S(1)} %get-tuple-element.26.metric_ref, bf16[8,4,8,3,32,128]{5,4,3,2,1,0:T(8,128)(2,1)} %bitcast.refs_0_), custom_call_target="tpu_custom_call" | custom-call | tf_op jit(solution)/shard_map/cond/branch_0_fun/gather_exchange/pallas_call | solution.py:277
  178.3 0.4 collective-permute-start
  178.7 1.2 half_exchange.2.before_ref
  179.9 1.1 collective-permute-done.got_ref
  181.0 2.0 rest_exchange.2
  183.2 2.9 %collective-permute-start.11 = (f32[128,512]{1,0:T(8,128)S(1)}, f32[128,512]{1,0:T(8,128)S(1)}, u32[]{:S(2)}, u32[]{:S(2)}) collective-permute-start(f32[128,512]{1,0:T(8,128)S(1)} %get-tuple-element.48), channel_id=1, source_target_pairs={{0,2},{1,3},{2,0},{3,1},{4,6},{5,7},{6,4},{7,5},{8,10},{9,11},{10,... | collective-permute-start | bytes 786440 | tf_op jit(solution)/shard_map/ppermute | solution.py:379
  186.1 0.4 collective-permute-start.12
  186.5 2.3 %collective-permute-start.13 = (f32[128,512]{1,0:T(8,128)S(1)}, f32[128,512]{1,0:T(8,128)S(1)}, u32[]{:S(2)}, u32[]{:S(2)}) collective-permute-start(f32[128,512]{1,0:T(8,128)S(1)} %get-tuple-element.50), channel_id=1, source_target_pairs={{0,3},{1,0},{2,1},{3,2},{4,7},{5,4},{6,5},{7,6},{8,11},{9,8},{10,9... | collective-permute-start | bytes 786440 | tf_op jit(solution)/shard_map/ppermute | solution.py:379
  188.8 3.6 %collective-permute-done.11 = f32[128,512]{1,0:T(8,128)S(1)} collective-permute-done((f32[128,512]{1,0:T(8,128)S(1)}, f32[128,512]{1,0:T(8,128)S(1)}, u32[]{:S(2)}, u32[]{:S(2)}) %collective-permute-start.11) | collective-permute-done | bytes 262176 | tf_op jit(solution)/shard_map/ppermute | solution.py:379
  192.4 6.3 %collective-permute-done.12 = f32[128,512]{1,0:T(8,128)S(1)} collective-permute-done((f32[128,512]{1,0:T(8,128)S(1)}, f32[128,512]{1,0:T(8,128)S(1)}, u32[]{:S(2)}, u32[]{:S(2)}) %collective-permute-start.12) | collective-permute-done | bytes 262176 | tf_op jit(solution)/shard_map/ppermute | solution.py:379
  198.6 0.7 add_convert_fusion
  (15 shorter events, 0.1 us)
Async XLA Ops:
  10.7 16.6 %copy-start.1 = (s32[32,8]{1,0:T(8,128)S(1)}, s32[32,8]{1,0:T(8,128)}, u32[]{:S(2)}) copy-start(s32[32,8]{1,0:T(8,128)} %get-tuple-element.44) | copy-start | bytes 3076
  10.8 159.2 %copy-start = (bf16[512,512]{1,0:T(8,128)(2,1)S(1)}, bf16[512,512]{1,0:T(8,128)(2,1)}, u32[]{:S(2)}) copy-start(bf16[512,512]{1,0:T(8,128)(2,1)} %param.11) | copy-start | bytes 1572868
  10.8 159.2 %all-to-all-start.1 = ((bf16[256,3,32,128]{3,2,1,0:T(8,128)(2,1)}), bf16[256,3,32,128]{3,2,1,0:T(8,128)(2,1)}, u32[]{:S(2)}, u32[]{:S(2)}) async-start(bf16[256,3,32,128]{3,2,1,0:T(8,128)(2,1)} %bitcast.42), calls=%async_computation.1 | async-start | bytes 12582912 | tf_op jit(solution)/shard_map/all_to_all | solution.py:357
  27.3 3.1 %collective-permute-start.2 = (s32[32,8]{1,0:T(8,128)S(1)}, s32[32,8]{1,0:T(8,128)S(1)}, u32[]{:S(2)}, u32[]{:S(2)}) collective-permute-start(s32[32,8]{1,0:T(8,128)S(1)} %copy-done.1), channel_id=1, source_target_pairs={{0,4},{4,0},{1,5},{5,1},{2,6},{6,2},{3,7},{7,3},{8,12},{12,8},{9,1... | collective-permute-start | bytes 3080 | tf_op jit(solution)/shard_map/ppermute | solution.py:332
  30.5 14.2 %collective-permute-start.5 = (s32[2,8,8]{2,1,0:T(8,128)S(1)}, s32[2,8,8]{2,1,0:T(8,128)S(1)}, u32[]{:S(2)}, u32[]{:S(2)}) collective-permute-start(s32[2,8,8]{2,1,0:T(8,128)S(1)} %get-tuple-element.66), channel_id=1, source_target_pairs={{0,192},{64,0},{128,64},{192,128},{1,193},{65,1},{129,65},{193,129... | collective-permute-start | bytes 1544 | tf_op jit(solution)/shard_map/ppermute | solution.py:337
  31.3 13.4 %collective-permute-start.4 = (s32[2,8,8]{2,1,0:T(8,128)S(1)}, s32[2,8,8]{2,1,0:T(8,128)S(1)}, u32[]{:S(2)}, u32[]{:S(2)}) collective-permute-start(s32[2,8,8]{2,1,0:T(8,128)S(1)} %get-tuple-element.67), channel_id=1, source_target_pairs={{0,128},{64,192},{128,0},{192,64},{1,129},{65,193},{129,1},{193,65... | collective-permute-start | bytes 1544 | tf_op jit(solution)/shard_map/ppermute | solution.py:337
  31.9 12.8 %collective-permute-start.3 = (s32[2,8,8]{2,1,0:T(8,128)S(1)}, s32[2,8,8]{2,1,0:T(8,128)S(1)}, u32[]{:S(2)}, u32[]{:S(2)}) collective-permute-start(s32[2,8,8]{2,1,0:T(8,128)S(1)} %get-tuple-element.68), channel_id=1, source_target_pairs={{0,64},{64,128},{128,192},{192,0},{1,65},{65,129},{129,193},{193,1... | collective-permute-start | bytes 1544 | tf_op jit(solution)/shard_map/ppermute | solution.py:337
  44.8 6.6 %collective-permute-start.9 = (s32[4,2,8]{2,1,0:T(2,128)S(1)}, s32[4,2,8]{2,1,0:T(2,128)S(1)}, u32[]{:S(2)}, u32[]{:S(2)}) collective-permute-start(s32[4,2,8]{2,1,0:T(2,128)S(1)} %bitcast.64), channel_id=1, source_target_pairs={{0,32},{4,4},{8,40},{12,12},{16,48},{20,20},{24,56},{28,28},{32,0}... | collective-permute-start | bytes 776 | tf_op jit(solution)/shard_map/ppermute | solution.py:343
  45.4 116.8 %collective-permute-start.6 = (s32[4,2,8]{2,1,0:T(2,128)S(1)}, s32[4,2,8]{2,1,0:T(2,128)S(1)}, u32[]{:S(2)}, u32[]{:S(2)}) collective-permute-start(s32[4,2,8]{2,1,0:T(2,128)S(1)} %bitcast.63), channel_id=1, source_target_pairs={{0,8},{4,44},{8,16},{12,52},{16,24},{20,60},{24,32},{28,4},{32,40}... | collective-permute-start | bytes 776 | tf_op jit(solution)/shard_map/ppermute | solution.py:343
  49.4 112.8 %collective-permute-start.8 = (s32[4,2,8]{2,1,0:T(2,128)S(1)}, s32[4,2,8]{2,1,0:T(2,128)S(1)}, u32[]{:S(2)}, u32[]{:S(2)}) collective-permute-start(s32[4,2,8]{2,1,0:T(2,128)S(1)} %bitcast.62), channel_id=1, source_target_pairs={{0,24},{4,60},{8,32},{12,4},{16,40},{20,12},{24,48},{28,20},{32,56... | collective-permute-start | bytes 776 | tf_op jit(solution)/shard_map/ppermute | solution.py:343
  51.2 111.0 %collective-permute-start.7 = (s32[4,2,8]{2,1,0:T(2,128)S(1)}, s32[4,2,8]{2,1,0:T(2,128)S(1)}, u32[]{:S(2)}, u32[]{:S(2)}) collective-permute-start(s32[4,2,8]{2,1,0:T(2,128)S(1)} %bitcast.61), channel_id=1, source_target_pairs={{0,16},{4,52},{8,24},{12,60},{16,32},{20,4},{24,40},{28,12},{32,48... | collective-permute-start | bytes 776 | tf_op jit(solution)/shard_map/ppermute | solution.py:343
  162.3 6.3 %collective-permute-start.10 = (s32[4,4,2,8]{3,2,1,0:T(2,128)S(1)}, s32[4,4,2,8]{3,2,1,0:T(2,128)S(1)}, u32[]{:S(2)}, u32[]{:S(2)}) collective-permute-start(s32[4,4,2,8]{3,2,1,0:T(2,128)S(1)} %pad_add_fusion.2), channel_id=1, source_target_pairs={{0,4},{4,0},{1,5},{5,1},{2,6},{6,2},{3,7},{7,3},{8,12},{12,8},{9,1... | collective-permute-start | bytes 3080 | tf_op jit(solution)/shard_map/ppermute | solution.py:345
  178.3 2.7 %collective-permute-start = (f32[512,512]{1,0:T(8,128)S(1)}, f32[512,512]{1,0:T(8,128)S(1)}, u32[]{:S(2)}, u32[]{:S(2)}) collective-permute-start(f32[512,512]{1,0:T(8,128)S(1)} %get-tuple-element.29), channel_id=1, source_target_pairs={{0,4},{4,0},{1,5},{5,1},{2,6},{6,2},{3,7},{7,3},{8,12},{12,8},{9,1... | collective-permute-start | bytes 3145736 | tf_op jit(solution)/shard_map/cond/branch_0_fun/ppermute | solution.py:365
  183.2 9.2 %collective-permute-start.11 = (f32[128,512]{1,0:T(8,128)S(1)}, f32[128,512]{1,0:T(8,128)S(1)}, u32[]{:S(2)}, u32[]{:S(2)}) collective-permute-start(f32[128,512]{1,0:T(8,128)S(1)} %get-tuple-element.48), channel_id=1, source_target_pairs={{0,2},{1,3},{2,0},{3,1},{4,6},{5,7},{6,4},{7,5},{8,10},{9,11},{10,... | collective-permute-start | bytes 786440 | tf_op jit(solution)/shard_map/ppermute | solution.py:379
  186.1 12.5 %collective-permute-start.12 = (f32[128,512]{1,0:T(8,128)S(1)}, f32[128,512]{1,0:T(8,128)S(1)}, u32[]{:S(2)}, u32[]{:S(2)}) collective-permute-start(f32[128,512]{1,0:T(8,128)S(1)} %get-tuple-element.49), channel_id=1, source_target_pairs={{0,1},{1,2},{2,3},{3,0},{4,5},{5,6},{6,7},{7,4},{8,9},{9,10},{10,1... | collective-permute-start | bytes 786440 | tf_op jit(solution)/shard_map/ppermute | solution.py:379
  186.5 12.2 %collective-permute-start.13 = (f32[128,512]{1,0:T(8,128)S(1)}, f32[128,512]{1,0:T(8,128)S(1)}, u32[]{:S(2)}, u32[]{:S(2)}) collective-permute-start(f32[128,512]{1,0:T(8,128)S(1)} %get-tuple-element.50), channel_id=1, source_target_pairs={{0,3},{1,0},{2,1},{3,2},{4,7},{5,4},{6,5},{7,6},{8,11},{9,8},{10,9... | collective-permute-start | bytes 786440 | tf_op jit(solution)/shard_map/ppermute | solution.py:379
where the time goes:
time: 200 us; the launch traced here: 199 us
  waiting for transfers between devices  136 us (68%)
  starting transfers between devices  38.7 us (19%)
  Pallas kernels  22.1 us (11%)
    ppermute x4, waiting for transfers between devices, share_tags(): lax.ppermute(part(table, (depth + away + half * core) % along, 2), ('z',...  111 us
    all_to_all x1, starting transfers between devices, body(): main = lax.all_to_all(main, AWAY, split_axis=0, concat_axis=0, tiled=True)  16.5 us
    ppermute x3, waiting for transfers between devices, share_tags(): lax.ppermute(part(both, (column + away) % across, 1), 'x', steps)  12.2 us
    pallas_call x1, Pallas kernels, make_units(): pl.pallas_call(units_kernel, in_specs=[scalars] * 4 + [pl.BlockSpec(memor...  10.7 us
    ppermute x3, waiting for transfers between devices, body(): lax.ppermute(shares[away], 'y', [(k, (k + away) % 4) for k in range(4)])  9.86 us
    pallas_call x1, Pallas kernels, gather_exchange(): pl.pallas_call(gather_kernel, in_specs=[scalars, scalars, held] + [pl.Blo...  8.12 us
    ppermute x4, starting transfers between devices, share_tags(): lax.ppermute(part(table, (depth + away + half * core) % along, 2), ('z',...  6.47 us
    ppermute x3, starting transfers between devices, body(): lax.ppermute(shares[away], 'y', [(k, (k + away) % 4) for k in range(4)])  5.58 us
  transfers between devices with their start and end apart: 14, of which 7 were waited for; matrix products, arithmetic and copies ran while one was open for 0% of the time, Pallas kernels for 1%

commit v1 on v0

--- a/solution.py
+++ b/solution.py
@@ -374,10 +374,13 @@
 
     overflow = jnp.max(tags[:, SLOTS]) > MAIN
     shares = lax.cond(overflow, many, few, main, extra, tags, place, metric_inv)
-    total = shares[0]
-    for away in (2, 1, 3):
-        total += lax.ppermute(shares[away], "y", [(k, (k + away) % 4) for k in range(4)])
-    return total.astype(jnp.bfloat16)
+    own, right, far, left = shares
+    half = far.shape[0] // 2
+    up, down = [(k, (k + 1) % 4) for k in range(4)], [(k, (k + 3) % 4) for k in range(4)]
+    from_left, from_right = lax.ppermute(far[:half], "y", up), lax.ppermute(far[half:], "y", down)
+    right = jnp.concatenate([right[:half] + from_left, right[half:]])
+    left = jnp.concatenate([left[:half], left[half:] + from_right])
+    return (own + lax.ppermute(right, "y", up) + lax.ppermute(left, "y", down)).astype(jnp.bfloat16)
 
 
 def solution(mesh):

time: 200 us -> 262 us (1.31)
  blocking collectives: 0 us -> 61.7 us
    all_to_all x0 -> x1, blocking collectives: none -> 61.7 us  [many(): extra = lax.all_to_all(extra, AWAY, split_axis=0, concat_axis=0, tiled=True)]
    ppermute x3 -> x4, waiting for transfers between devices: 9.86 us -> 11.1 us  [the longest x1 4.5 us: body(): lax.ppermute(left, 'y', down)]
    ppermute x3 -> x4, starting transfers between devices: 5.58 us -> 4.78 us  [the longest x1 2.95 us: body(): lax.ppermute(left, 'y', down)]
  transfers between devices with their start and end apart: 14 -> 15, of which waited for: 7 -> 8; matrix products, arithmetic and copies ran while one was open for 0% -> 0% of each run, Pallas kernels for 1% -> 0%
where the time goes in v1:
time: 262 us
  waiting for transfers between devices  137 us (52%)
  blocking collectives  61.7 us (24%)
  starting transfers between devices  37.6 us (14%)
  Pallas kernels  22.6 us (9%)
    ppermute x4, waiting for transfers between devices, share_tags(): lax.ppermute(part(table, (depth + away + half * core) % along, 2), ('z',...  111 us
    all_to_all x1, blocking collectives, many(): extra = lax.all_to_all(extra, AWAY, split_axis=0, concat_axis=0, tiled=True)  61.7 us
    all_to_all x1, starting transfers between devices, body(): main = lax.all_to_all(main, AWAY, split_axis=0, concat_axis=0, tiled=True)  16.6 us
    ppermute x3, waiting for transfers between devices, share_tags(): lax.ppermute(part(both, (column + away) % across, 1), 'x', steps)  12.2 us
    pallas_call x1, Pallas kernels, make_units(): pl.pallas_call(units_kernel, in_specs=[scalars] * 4 + [pl.BlockSpec(memor...  10.8 us
    pallas_call x1, Pallas kernels, gather_exchange(): pl.pallas_call(gather_kernel, in_specs=[scalars, scalars, held] + [pl.Blo...  8.65 us
    ppermute x4, starting transfers between devices, share_tags(): lax.ppermute(part(table, (depth + away + half * core) % along, 2), ('z',...  6.47 us
    ppermute x1, starting transfers between devices, share_tags(): return jnp.stack([rows, lax.ppermute(rows, 'c', swap)])  5.42 us
  transfers between devices with their start and end apart: 15, of which 8 were waited for; matrix products, arithmetic and copies ran while one was open for 0% of the time, Pallas kernels for 0%

profile of v1, /device:TPU:1, one launch (start us, length us, event | category | flops | bytes accessed | tf_op | source)
XLA Modules:
  0.0 262.0 jit_solution(693834336530772481)
XLA Ops:
  0.0 10.8 %units.1 = (bf16[2,4,4,8,3,32,128]{6,5,4,3,2,1,0:T(8,128)(2,1)}, bf16[2,4,4,8,1,32,128]{6,5,4,3,2,1,0:T(8,128)(2,1)S(1)}, s32[32,8]{1,0:T(8,128)}) custom-call(s32[48]{0:T(128)} %bitcast.65, s32[48]{0:T(128)} %row_ref.1, s32[48]{0:T(128)} %aux_ref.1, s32[48]{0:T(128)} %ao_ref.1, bf16[48,16,4096]{2,1,0:T(8,128)(2,1)} %three_ref.1, bf16[32,19968]{1,0:T(8,128)(2,1)} %coef_ref.1), custom_call_target="tpu_custom_call" | custom-call | tf_op jit(solution)/shard_map/units/pallas_call | solution.py:141
  10.8 0.0 copy-start.1
  10.8 0.0 copy-start
  10.8 16.6 %all-to-all-start.1 = ((bf16[256,3,32,128]{3,2,1,0:T(8,128)(2,1)}), bf16[256,3,32,128]{3,2,1,0:T(8,128)(2,1)}, u32[]{:S(2)}, u32[]{:S(2)}) async-start(bf16[256,3,32,128]{3,2,1,0:T(8,128)(2,1)} %bitcast.42), calls=%async_computation.1 | async-start | bytes 12582912 | tf_op jit(solution)/shard_map/all_to_all | solution.py:357
  27.4 2.3 collective-permute-start.2
  29.7 0.8 collective-permute-done.2
  30.5 0.8 collective-permute-start.5
  31.3 0.6 collective-permute-start.4
  31.9 0.6 collective-permute-start.3
  32.5 12.2 %collective-permute-done.5 = s32[2,8,8]{2,1,0:T(8,128)S(1)} collective-permute-done((s32[2,8,8]{2,1,0:T(8,128)S(1)}, s32[2,8,8]{2,1,0:T(8,128)S(1)}, u32[]{:S(2)}, u32[]{:S(2)}) %collective-permute-start.5) | collective-permute-done | bytes 544 | tf_op jit(solution)/shard_map/ppermute | solution.py:337
  44.8 0.7 collective-permute-start.9
  45.4 4.0 %collective-permute-start.6 = (s32[4,2,8]{2,1,0:T(2,128)S(1)}, s32[4,2,8]{2,1,0:T(2,128)S(1)}, u32[]{:S(2)}, u32[]{:S(2)}) collective-permute-start(s32[4,2,8]{2,1,0:T(2,128)S(1)} %bitcast.63), channel_id=1, source_target_pairs={{0,8},{4,44},{8,16},{12,52},{16,24},{20,60},{24,32},{28,4},{32,40}... | collective-permute-start | bytes 776 | tf_op jit(solution)/shard_map/ppermute | solution.py:343
  49.5 1.8 collective-permute-start.8
  51.3 0.1 pad_add_fusion.3
  51.3 110.9 %collective-permute-done.6 = s32[4,2,8]{2,1,0:T(2,128)S(1)} collective-permute-done((s32[4,2,8]{2,1,0:T(2,128)S(1)}, s32[4,2,8]{2,1,0:T(2,128)S(1)}, u32[]{:S(2)}, u32[]{:S(2)}) %collective-permute-start.6) | collective-permute-done | bytes 288 | tf_op jit(solution)/shard_map/ppermute | solution.py:343
  162.3 5.4 %collective-permute-start.10 = (s32[4,4,2,8]{3,2,1,0:T(2,128)S(1)}, s32[4,4,2,8]{3,2,1,0:T(2,128)S(1)}, u32[]{:S(2)}, u32[]{:S(2)}) collective-permute-start(s32[4,4,2,8]{3,2,1,0:T(2,128)S(1)} %pad_add_fusion.2), channel_id=1, source_target_pairs={{0,4},{4,0},{1,5},{5,1},{2,6},{6,2},{3,7},{7,3},{8,12},{12,8},{9,1... | collective-permute-start | bytes 3080 | tf_op jit(solution)/shard_map/ppermute | solution.py:345
  167.7 0.8 collective-permute-done.10
  168.6 0.7 slice_reduce_fusion
  170.0 75.3 %conditional.1 = ((f32[128,512]{1,0:T(8,128)S(1)}, f32[128,512]{1,0:T(8,128)S(1)}, f32[128,512]{1,0:T(8,128)S(1)}, f32[128,512]{1,0:T(8,128)S(1)})) conditional(s32[]{:T(128)} %convert_element_type.6, (bf16[256,3,32,128]{3,2,1,0:T(8,128)(2,1)}, s32[64,8]{1,0:T(8,128)S(1)}, s32[4]{0:T(128)S(1)}, bf16[512,512]{1,0:T(8,128)(2,1)S(1)}) %tuple.30, ...), branch_computations={%region_1.2_spmd, %region_2.3_spmd} | conditional | flops 1073741824 | bytes 13631536 | solution.py:376
  170.2 61.7 %all_to_all.9 = bf16[256,1,32,128]{3,2,1,0:T(8,128)(2,1)S(1)} all-to-all(bf16[256,1,32,128]{3,2,1,0:T(8,128)(2,1)S(1)} %bitcast.43), channel_id=1, replica_groups=mesh['x'=4,'z'=8,'c'=2,'y'=4] {'c','x','y','z'}, dimensions={0} | all-to-all | bytes 4194304 | tf_op jit(solution)/shard_map/cond/branch_1_fun/all_to_all | solution.py:372
  231.9 8.7 %gather_exchange.3 = (bf16[2,512,1024]{2,1,0:T(8,128)(2,1)S(1)}, f32[512,512]{1,0:T(8,128)S(1)}) custom-call(s32[64,8]{1,0:T(8,128)S(1)} %get-tuple-element.31.tag_ref, s32[4]{0:T(128)S(1)} %get-tuple-element.30.place_ref, bf16[512,512]{1,0:T(8,128)(2,1)S(1)} %get-tuple-element.32.metric_ref, bf16[8,4,8,3,32,128]{5,4,3,2,1,0:T(8,128)(2,1)} %bitcast.1.refs_0_, ...), custom_call_target="tpu_custom_call" | custom-call | tf_op jit(solution)/shard_map/cond/branch_1_fun/gather_exchange/pallas_call | solution.py:277
  240.6 0.1 collective-permute-start.1
  240.7 1.2 half_exchange.3.before_ref
  241.9 1.4 collective-permute-done.1.got_ref
  243.3 2.0 rest_exchange.3
  245.3 1.7 collective-permute-start.13
  247.0 3.3 %collective-permute-done.13 = f32[64,512]{1,0:T(8,128)S(1)} collective-permute-done((f32[64,512]{1,0:T(8,128)S(1)}, f32[64,512]{1,0:T(8,128)S(1)}, u32[]{:S(2)}, u32[]{:S(2)}) %collective-permute-start.13) | collective-permute-done | bytes 131104 | tf_op jit(solution)/shard_map/ppermute | solution.py:380
  250.4 3.0 %collective-permute-start.14 = (f32[128,512]{1,0:T(8,128)S(1)}, f32[128,512]{1,0:T(8,128)S(1)}, u32[]{:S(2)}, u32[]{:S(2)}) collective-permute-start(f32[128,512]{1,0:T(8,128)S(1)} %pad_maximum_fusion.1), channel_id=1, source_target_pairs={{0,3},{1,0},{2,1},{3,2},{4,7},{5,4},{6,5},{7,6},{8,11},{9,8},{10,9... | collective-permute-start | bytes 786440 | tf_op jit(solution)/shard_map/ppermute | solution.py:383
  253.4 0.1 collective-permute-start.12
  253.5 4.5 %collective-permute-done.14 = f32[128,512]{1,0:T(8,128)S(1)} collective-permute-done((f32[128,512]{1,0:T(8,128)S(1)}, f32[128,512]{1,0:T(8,128)S(1)}, u32[]{:S(2)}, u32[]{:S(2)}) %collective-permute-start.14) | collective-permute-done | bytes 262176 | tf_op jit(solution)/shard_map/ppermute | solution.py:383
  258.0 3.3 %collective-permute-done.12 = f32[128,512]{1,0:T(8,128)S(1)} collective-permute-done((f32[128,512]{1,0:T(8,128)S(1)}, f32[128,512]{1,0:T(8,128)S(1)}, u32[]{:S(2)}, u32[]{:S(2)}) %collective-permute-start.12) | collective-permute-done | bytes 262176 | tf_op jit(solution)/shard_map/ppermute | solution.py:383
  261.3 0.7 add_convert_fusion
  (23 shorter events, 0.2 us)
Async XLA Ops:
  10.8 16.6 %copy-start.1 = (s32[32,8]{1,0:T(8,128)S(1)}, s32[32,8]{1,0:T(8,128)}, u32[]{:S(2)}) copy-start(s32[32,8]{1,0:T(8,128)} %get-tuple-element.44) | copy-start | bytes 3076
  10.8 159.2 %copy-start = (bf16[512,512]{1,0:T(8,128)(2,1)S(1)}, bf16[512,512]{1,0:T(8,128)(2,1)}, u32[]{:S(2)}) copy-start(bf16[512,512]{1,0:T(8,128)(2,1)} %param.11) | copy-start | bytes 1572868
  10.8 159.2 %all-to-all-start.1 = ((bf16[256,3,32,128]{3,2,1,0:T(8,128)(2,1)}), bf16[256,3,32,128]{3,2,1,0:T(8,128)(2,1)}, u32[]{:S(2)}, u32[]{:S(2)}) async-start(bf16[256,3,32,128]{3,2,1,0:T(8,128)(2,1)} %bitcast.42), calls=%async_computation.1 | async-start | bytes 12582912 | tf_op jit(solution)/shard_map/all_to_all | solution.py:357
  27.4 3.1 %collective-permute-start.2 = (s32[32,8]{1,0:T(8,128)S(1)}, s32[32,8]{1,0:T(8,128)S(1)}, u32[]{:S(2)}, u32[]{:S(2)}) collective-permute-start(s32[32,8]{1,0:T(8,128)S(1)} %copy-done.1), channel_id=1, source_target_pairs={{0,4},{4,0},{1,5},{5,1},{2,6},{6,2},{3,7},{7,3},{8,12},{12,8},{9,1... | collective-permute-start | bytes 3080 | tf_op jit(solution)/shard_map/ppermute | solution.py:332
  30.5 14.2 %collective-permute-start.5 = (s32[2,8,8]{2,1,0:T(8,128)S(1)}, s32[2,8,8]{2,1,0:T(8,128)S(1)}, u32[]{:S(2)}, u32[]{:S(2)}) collective-permute-start(s32[2,8,8]{2,1,0:T(8,128)S(1)} %get-tuple-element.72), channel_id=1, source_target_pairs={{0,192},{64,0},{128,64},{192,128},{1,193},{65,1},{129,65},{193,129... | collective-permute-start | bytes 1544 | tf_op jit(solution)/shard_map/ppermute | solution.py:337
  31.3 13.4 %collective-permute-start.4 = (s32[2,8,8]{2,1,0:T(8,128)S(1)}, s32[2,8,8]{2,1,0:T(8,128)S(1)}, u32[]{:S(2)}, u32[]{:S(2)}) collective-permute-start(s32[2,8,8]{2,1,0:T(8,128)S(1)} %get-tuple-element.73), channel_id=1, source_target_pairs={{0,128},{64,192},{128,0},{192,64},{1,129},{65,193},{129,1},{193,65... | collective-permute-start | bytes 1544 | tf_op jit(solution)/shard_map/ppermute | solution.py:337
  31.9 12.8 %collective-permute-start.3 = (s32[2,8,8]{2,1,0:T(8,128)S(1)}, s32[2,8,8]{2,1,0:T(8,128)S(1)}, u32[]{:S(2)}, u32[]{:S(2)}) collective-permute-start(s32[2,8,8]{2,1,0:T(8,128)S(1)} %get-tuple-element.74), channel_id=1, source_target_pairs={{0,64},{64,128},{128,192},{192,0},{1,65},{65,129},{129,193},{193,1... | collective-permute-start | bytes 1544 | tf_op jit(solution)/shard_map/ppermute | solution.py:337
  44.8 6.6 %collective-permute-start.9 = (s32[4,2,8]{2,1,0:T(2,128)S(1)}, s32[4,2,8]{2,1,0:T(2,128)S(1)}, u32[]{:S(2)}, u32[]{:S(2)}) collective-permute-start(s32[4,2,8]{2,1,0:T(2,128)S(1)} %bitcast.64), channel_id=1, source_target_pairs={{0,32},{4,4},{8,40},{12,12},{16,48},{20,20},{24,56},{28,28},{32,0}... | collective-permute-start | bytes 776 | tf_op jit(solution)/shard_map/ppermute | solution.py:343
  45.4 116.8 %collective-permute-start.6 = (s32[4,2,8]{2,1,0:T(2,128)S(1)}, s32[4,2,8]{2,1,0:T(2,128)S(1)}, u32[]{:S(2)}, u32[]{:S(2)}) collective-permute-start(s32[4,2,8]{2,1,0:T(2,128)S(1)} %bitcast.63), channel_id=1, source_target_pairs={{0,8},{4,44},{8,16},{12,52},{16,24},{20,60},{24,32},{28,4},{32,40}... | collective-permute-start | bytes 776 | tf_op jit(solution)/shard_map/ppermute | solution.py:343
  49.5 112.8 %collective-permute-start.8 = (s32[4,2,8]{2,1,0:T(2,128)S(1)}, s32[4,2,8]{2,1,0:T(2,128)S(1)}, u32[]{:S(2)}, u32[]{:S(2)}) collective-permute-start(s32[4,2,8]{2,1,0:T(2,128)S(1)} %bitcast.62), channel_id=1, source_target_pairs={{0,24},{4,60},{8,32},{12,4},{16,40},{20,12},{24,48},{28,20},{32,56... | collective-permute-start | bytes 776 | tf_op jit(solution)/shard_map/ppermute | solution.py:343
  51.3 111.0 %collective-permute-start.7 = (s32[4,2,8]{2,1,0:T(2,128)S(1)}, s32[4,2,8]{2,1,0:T(2,128)S(1)}, u32[]{:S(2)}, u32[]{:S(2)}) collective-permute-start(s32[4,2,8]{2,1,0:T(2,128)S(1)} %bitcast.61), channel_id=1, source_target_pairs={{0,16},{4,52},{8,24},{12,60},{16,32},{20,4},{24,40},{28,12},{32,48... | collective-permute-start | bytes 776 | tf_op jit(solution)/shard_map/ppermute | solution.py:343
  162.3 6.3 %collective-permute-start.10 = (s32[4,4,2,8]{3,2,1,0:T(2,128)S(1)}, s32[4,4,2,8]{3,2,1,0:T(2,128)S(1)}, u32[]{:S(2)}, u32[]{:S(2)}) collective-permute-start(s32[4,4,2,8]{3,2,1,0:T(2,128)S(1)} %pad_add_fusion.2), channel_id=1, source_target_pairs={{0,4},{4,0},{1,5},{5,1},{2,6},{6,2},{3,7},{7,3},{8,12},{12,8},{9,1... | collective-permute-start | bytes 3080 | tf_op jit(solution)/shard_map/ppermute | solution.py:345
  240.6 2.7 %collective-permute-start.1 = (f32[512,512]{1,0:T(8,128)S(1)}, f32[512,512]{1,0:T(8,128)S(1)}, u32[]{:S(2)}, u32[]{:S(2)}) collective-permute-start(f32[512,512]{1,0:T(8,128)S(1)} %get-tuple-element.36), channel_id=1, source_target_pairs={{0,4},{4,0},{1,5},{5,1},{2,6},{6,2},{3,7},{7,3},{8,12},{12,8},{9,1... | collective-permute-start | bytes 3145736 | tf_op jit(solution)/shard_map/cond/branch_1_fun/ppermute | solution.py:365
  245.3 5.0 %collective-permute-start.13 = (f32[64,512]{1,0:T(8,128)S(1)}, f32[64,512]{1,0:T(8,128)S(1)}, u32[]{:S(2)}, u32[]{:S(2)}) collective-permute-start(f32[64,512]{1,0:T(8,128)S(1)} %get-tuple-element.64), channel_id=1, source_target_pairs={{0,3},{1,0},{2,1},{3,2},{4,7},{5,4},{6,5},{7,6},{8,11},{9,8},{10,9... | collective-permute-start | bytes 393224 | tf_op jit(solution)/shard_map/ppermute | solution.py:380
  247.0 6.3 %collective-permute-start.11 = (f32[64,512]{1,0:T(8,128)S(1)}, f32[64,512]{1,0:T(8,128)S(1)}, u32[]{:S(2)}, u32[]{:S(2)}) collective-permute-start(f32[64,512]{1,0:T(8,128)S(1)} %get-tuple-element.63), channel_id=1, source_target_pairs={{0,1},{1,2},{2,3},{3,0},{4,5},{5,6},{6,7},{7,4},{8,9},{9,10},{10,1... | collective-permute-start | bytes 393224 | tf_op jit(solution)/shard_map/ppermute | solution.py:380
  250.4 7.6 %collective-permute-start.14 = (f32[128,512]{1,0:T(8,128)S(1)}, f32[128,512]{1,0:T(8,128)S(1)}, u32[]{:S(2)}, u32[]{:S(2)}) collective-permute-start(f32[128,512]{1,0:T(8,128)S(1)} %pad_maximum_fusion.1), channel_id=1, source_target_pairs={{0,3},{1,0},{2,1},{3,2},{4,7},{5,4},{6,5},{7,6},{8,11},{9,8},{10,9... | collective-permute-start | bytes 786440 | tf_op jit(solution)/shard_map/ppermute | solution.py:383
  253.4 7.9 %collective-permute-start.12 = (f32[128,512]{1,0:T(8,128)S(1)}, f32[128,512]{1,0:T(8,128)S(1)}, u32[]{:S(2)}, u32[]{:S(2)}) collective-permute-start(f32[128,512]{1,0:T(8,128)S(1)} %pad_maximum_fusion), channel_id=1, source_target_pairs={{0,1},{1,2},{2,3},{3,0},{4,5},{5,6},{6,7},{7,4},{8,9},{9,10},{10,1... | collective-permute-start | bytes 786440 | tf_op jit(solution)/shard_map/ppermute | solution.py:383
